TPU v7x, 256 devices: a whole 4x4x8 slice. The times are simulated.
256 devices in a mesh: leaf: 16 (over x, y), row: 16 (over z, core).
Axes of the slice: x: 4, y: 4, z: 8, core: 2. Of those that a mesh axis runs over, the one named last changes fastest.
Arguments:
- rhs: bfloat16 [6, 16, 512, 256], P(None, 'leaf', 'row'), may hold values from -6 to 6
- diag_inverse: bfloat16 [16, 6, 512, 512], P('leaf'), as said below
- factor: bfloat16 [16, 178, 512, 512], P('leaf', None, 'row'), as said below
- widths: int32 [6, 16], P(None, 'leaf'), may hold values from 64 to 512, as said below
- structure: int32 [16, 178], P('leaf'), may hold values from 0 to 1, as said below
Outputs:
- forward_solution: bfloat16 [6, 16, 512, 256], P(None, 'leaf', 'row')
- adjoint_solution: bfloat16 [6, 16, 512, 256], P(None, 'leaf', 'row')
Inputs may be any that keep to these rules, and one draw needn't show every extreme that they name: `widths`: every draw has a supernode of exactly 512 columns and one of exactly one eighth of 512 columns. `structure`: 1 where the block is present. Each diag_inverse[j, l] is lower triangular with diagonal entries from 0.5 to 1. `factor`: dense blocks of independent entries.
All inputs are finite; a program needn't handle non-finite values.
Results may differ from a plain program's by a relative error of at most 0.017.
Values may be sent and summed in bfloat16 or wider, within the bound.
A program may use at most 64 MiB of HBM per device.

v0:
```python
import jax
import jax.numpy as jnp
from jax import lax
from jax.sharding import PartitionSpec as P


def group_size(level_now, leaf_count):
    return min(2**level_now, leaf_count)


def block_offsets(levels, leaf_count):
    offset_table = {}
    cursor = 0
    for source_level in range(levels):
        for target_level in range(source_level + 1, levels):
            offset_table[source_level, target_level] = cursor
            cursor += group_size(target_level, leaf_count)
    return offset_table


def blocks_after(level_now, levels, leaf_count):
    return sum(
        (group_size(target_level, leaf_count) for target_level in range(level_now + 1, levels))
    )


def contract_rows(left_side, right_side):
    return lax.dot_general(
        left_side, right_side, (((0,), (0,)), ((), ())), preferred_element_type=jnp.float32
    )


def apply_columns(matrix, shard_piece):
    return jnp.dot(matrix, shard_piece, preferred_element_type=jnp.float32)


def group_reduce(partials, group_span, leaf_count, leaf_index):
    group_base = leaf_index // group_span * group_span
    spread = jnp.zeros((leaf_count,) + partials.shape[1:], jnp.float32)
    spread = lax.dynamic_update_slice_in_dim(spread, partials, group_base, 0)
    return lax.psum_scatter(
        spread.astype(jnp.bfloat16), "leaf", scatter_dimension=0, tiled=True
    ).astype(jnp.float32)[0]


def group_collect(own_block, group_span, leaf_index):
    everyone = lax.all_gather(own_block[None], "leaf", axis=0, tiled=True)
    group_base = leaf_index // group_span * group_span
    return lax.dynamic_slice_in_dim(everyone, group_base, group_span, 0)


def adjoint_level(flat_blocks, flat_values, own_full, full_mask, block_mask, inverse_cols):
    pulled = lax.psum(contract_rows(flat_blocks, flat_values).astype(jnp.bfloat16), "row").astype(
        jnp.float32
    )
    reduced_full = (full_mask[:, None] * (own_full.astype(jnp.float32) - pulled)).astype(
        jnp.bfloat16
    )
    solved = contract_rows(inverse_cols, reduced_full)
    return (block_mask[:, None] * solved).astype(jnp.bfloat16)


def shards(rhs, diag_inverse, factor, widths, structure):
    leaf_count = lax.axis_size("leaf")
    leaf_index = lax.axis_index("leaf")
    row_index = lax.axis_index("row")
    levels = rhs.shape[0]
    block_rows = rhs.shape[2]
    columns = rhs.shape[3]
    full_width = factor.shape[3]
    inverse = diag_inverse[0]
    blocks = factor[0]
    weights = structure[0].astype(jnp.float32)
    own_rows = row_index * block_rows
    positions = jnp.arange(full_width, dtype=jnp.int32)
    full_masks = (positions[None, :] < widths).astype(jnp.float32)
    block_masks = lax.dynamic_slice_in_dim(full_masks, own_rows, block_rows, 1)
    offset_table = block_offsets(levels, leaf_count)
    pending = {}
    for target_level in range(1, levels):
        pending[target_level] = jnp.zeros(
            (group_size(target_level, leaf_count), block_rows, columns), jnp.float32
        )
    forward_blocks = []
    forward_full = []
    for level_now in range(levels):
        if level_now > 0:
            incoming = group_reduce(
                pending[level_now], group_size(level_now, leaf_count), leaf_count, leaf_index
            )
        else:
            incoming = jnp.zeros((block_rows, columns), jnp.float32)
        residual = (
            block_masks[level_now][:, None] * (rhs[level_now, 0].astype(jnp.float32) - incoming)
        ).astype(jnp.bfloat16)
        solve_rows = inverse[level_now]
        folded = apply_columns(solve_rows, lax.all_gather(residual, "row", axis=0, tiled=True))
        solved_full = (full_masks[level_now][:, None] * folded).astype(jnp.bfloat16)
        solved_block = lax.dynamic_slice_in_dim(solved_full, own_rows, block_rows, 0)
        forward_blocks.append(solved_block)
        forward_full.append(solved_full)
        if level_now + 1 < levels:
            first_block = offset_table[level_now, level_now + 1]
            block_count = blocks_after(level_now, levels, leaf_count)
            chosen = blocks[first_block : first_block + block_count].reshape(
                block_count * block_rows, full_width
            )
            products = jnp.dot(chosen, solved_full, preferred_element_type=jnp.float32).reshape(
                block_count, block_rows, columns
            )
            products = products * weights[first_block : first_block + block_count][:, None, None]
            cursor = 0
            for target_level in range(level_now + 1, levels):
                group_span = group_size(target_level, leaf_count)
                pending[target_level] = (
                    pending[target_level] + products[cursor : cursor + group_span]
                )
                cursor += group_span
    gathered = {}
    adjoint_blocks = [None] * levels
    for level_now in reversed(range(levels)):
        inverse_cols = lax.dynamic_slice_in_dim(inverse[level_now], own_rows, block_rows, 1)
        if level_now + 1 == levels:
            solved = contract_rows(inverse_cols, forward_full[level_now])
            own_adjoint = (block_masks[level_now][:, None] * solved).astype(jnp.bfloat16)
        else:
            first_block = offset_table[level_now, level_now + 1]
            block_count = blocks_after(level_now, levels, leaf_count)
            stacked = jnp.concatenate(
                [gathered[upper_level] for upper_level in range(level_now + 1, levels)], 0
            )
            stacked = stacked * structure[0, first_block : first_block + block_count][
                :, None, None
            ].astype(jnp.bfloat16)
            flat_blocks = blocks[first_block : first_block + block_count].reshape(
                block_count * block_rows, full_width
            )
            flat_values = stacked.reshape(block_count * block_rows, columns)
            own_adjoint = adjoint_level(
                flat_blocks,
                flat_values,
                forward_full[level_now],
                full_masks[level_now],
                block_masks[level_now],
                inverse_cols,
            )
        adjoint_blocks[level_now] = own_adjoint
        if level_now > 0:
            gathered[level_now] = group_collect(
                own_adjoint, group_size(level_now, leaf_count), leaf_index
            )
    return (jnp.stack(forward_blocks)[:, None], jnp.stack(adjoint_blocks)[:, None])


def solution(mesh):
    placed = (
        P(None, "leaf", "row", None),
        P("leaf", None, None, None),
        P("leaf", None, "row", None),
        P(None, "leaf"),
        P("leaf", None),
    )
    return jax.shard_map(
        shards,
        mesh=mesh,
        in_specs=placed,
        out_specs=(P(None, "leaf", "row", None), P(None, "leaf", "row", None)),
        check_vma=False,
    )
```

profile of v0, /device:TPU:1, one launch (start us, length us, event | category | flops | bytes accessed | tf_op | source)
XLA Modules:
  0.0 1223.9 jit_solution(11152830773635222627)
XLA Ops:
  8.9 22.0 %all_gather.33 = bf16[512,256]{1,0:T(8,128)(2,1)S(1)} all-gather(bf16[32,256]{1,0:T(8,128)(2,1)S(1)} %fusion.72), channel_id=1, replica_groups=mesh['leaf'=16,'row'=16] {'row'}, dimensions={0}, use_global_device_ids=true | all-gather | bytes 278528 | tf_op jit(solution)/shard_map/all_gather | solution.py:97
  30.9 1.6 slice.219
  32.6 1.4 fusion
  34.9 1.1 copy-done
  36.8 1.5 slice.228
  38.4 71.6 %reduce-scatter.16.cloned.1.call-done = bf16[1,32,256]{2,1,0:T(8,128)(2,1)} async-done(((bf16[16,32,256]{2,1,0:T(8,128)(2,1)}), bf16[1,32,256]{2,1,0:T(8,128)(2,1)}) %reduce-scatter.16.cloned.1.call-update) | async-done | bytes 16400
  110.8 20.2 %all_gather.34 = bf16[512,256]{1,0:T(8,128)(2,1)S(1)} all-gather(bf16[32,256]{1,0:T(8,128)(2,1)S(1)} %fusion.71), channel_id=1, replica_groups=mesh['leaf'=16,'row'=16] {'row'}, dimensions={0}, use_global_device_ids=true | all-gather | bytes 278528 | tf_op jit(solution)/shard_map/all_gather | solution.py:97
  131.0 1.4 fusion.1
  133.1 1.7 convolution_bitcast_fusion.1
  134.8 2.9 copy.19
  137.7 1.5 broadcast_multiply_fusion.1
  139.3 1.1 copy-done.1
  142.1 2.5 slice.238
  144.7 69.2 %reduce-scatter.18.cloned.1.call-done = bf16[1,32,256]{2,1,0:T(8,128)(2,1)} async-done(((bf16[16,32,256]{2,1,0:T(8,128)(2,1)}), bf16[1,32,256]{2,1,0:T(8,128)(2,1)}) %reduce-scatter.18.cloned.1.call-update) | async-done | bytes 16400
  214.8 20.3 %all_gather.35 = bf16[512,256]{1,0:T(8,128)(2,1)S(1)} all-gather(bf16[32,256]{1,0:T(8,128)(2,1)S(1)} %fusion.69), channel_id=1, replica_groups=mesh['leaf'=16,'row'=16] {'row'}, dimensions={0}, use_global_device_ids=true | all-gather | bytes 278528 | tf_op jit(solution)/shard_map/all_gather | solution.py:97
  235.1 1.4 fusion.2
  237.2 1.6 convolution_bitcast_fusion
  238.8 2.8 copy.20
  241.6 1.5 broadcast_multiply_fusion.2
  246.0 2.3 slice.249
  248.5 69.3 %reduce-scatter.20.cloned.1.call-done = bf16[1,32,256]{2,1,0:T(8,128)(2,1)} async-done(((bf16[16,32,256]{2,1,0:T(8,128)(2,1)}), bf16[1,32,256]{2,1,0:T(8,128)(2,1)}) %reduce-scatter.20.cloned.1.call-update) | async-done | bytes 16400
  318.6 20.2 %all_gather.36 = bf16[512,256]{1,0:T(8,128)(2,1)S(1)} all-gather(bf16[32,256]{1,0:T(8,128)(2,1)S(1)} %fusion.67), channel_id=1, replica_groups=mesh['leaf'=16,'row'=16] {'row'}, dimensions={0}, use_global_device_ids=true | all-gather | bytes 278528 | tf_op jit(solution)/shard_map/all_gather | solution.py:97
  338.9 1.4 fusion.3
  341.0 1.5 convolution_bitcast_fusion.2
  342.5 2.6 copy.21
  345.1 1.4 broadcast_multiply_fusion.3
  347.5 2.2 fusion.21
  352.1 69.4 %reduce-scatter.22.cloned.1.call-done = bf16[1,32,256]{2,1,0:T(8,128)(2,1)} async-done(((bf16[16,32,256]{2,1,0:T(8,128)(2,1)}), bf16[1,32,256]{2,1,0:T(8,128)(2,1)}) %reduce-scatter.22.cloned.1.call-update) | async-done | bytes 16400
  422.3 20.3 %all_gather.37 = bf16[512,256]{1,0:T(8,128)(2,1)S(1)} all-gather(bf16[32,256]{1,0:T(8,128)(2,1)S(1)} %fusion.65), channel_id=1, replica_groups=mesh['leaf'=16,'row'=16] {'row'}, dimensions={0}, use_global_device_ids=true | all-gather | bytes 278528 | tf_op jit(solution)/shard_map/all_gather | solution.py:97
  442.6 1.4 fusion.4
  444.7 1.2 convolution_bitcast_fusion.3
  445.9 2.1 copy.22
  448.0 2.5 fusion.20
  451.1 3.5 fusion.86
  454.7 67.7 %reduce-scatter.24.cloned.1.call-done = bf16[1,32,256]{2,1,0:T(8,128)(2,1)} async-done(((bf16[16,32,256]{2,1,0:T(8,128)(2,1)}), bf16[1,32,256]{2,1,0:T(8,128)(2,1)}) %reduce-scatter.24.cloned.1.call-update) | async-done | bytes 16400
  523.2 20.2 %all_gather.38 = bf16[512,256]{1,0:T(8,128)(2,1)S(1)} all-gather(bf16[32,256]{1,0:T(8,128)(2,1)S(1)} %fusion.63), channel_id=1, replica_groups=mesh['leaf'=16,'row'=16] {'row'}, dimensions={0}, use_global_device_ids=true | all-gather | bytes 278528 | tf_op jit(solution)/shard_map/all_gather | solution.py:97
  543.4 1.4 fusion.5
  544.8 1.2 fusion.11
  546.1 18.0 %all-gather = bf16[512,256]{1,0:T(8,128)(2,1)S(1)} all-gather(bf16[32,256]{1,0:T(8,128)(2,1)S(1)} %fusion.11), channel_id=2, replica_groups=mesh['leaf'=16,'row'=16] {'leaf'}, dimensions={0}, use_global_device_ids=true | all-gather | bytes 278528 | tf_op jit(solution)/shard_map/all_gather | solution.py:47
  565.9 1.6 dynamic-slice_bitcast_fusion.4
  567.5 1.5 copy.23
  569.0 105.7 %all-reduce.11.cloned.1.call-done = bf16[512,256]{0,1:T(8,128)(2,1)} async-done(((bf16[512,256]{0,1:T(8,128)(2,1)}), bf16[512,256]{0,1:T(8,128)(2,1)}) %all-reduce.11.cloned.1.call-update) | async-done | bytes 262160 | tf_op jit(solution)/shard_map/psum | solution.py:53
  674.7 1.3 fusion.12
  676.1 18.5 %all-gather.1 = bf16[512,256]{1,0:T(8,128)(2,1)S(1)} all-gather(bf16[32,256]{1,0:T(8,128)(2,1)S(1)} %fusion.12), channel_id=3, replica_groups=mesh['leaf'=16,'row'=16] {'leaf'}, dimensions={0}, use_global_device_ids=true | all-gather | bytes 278528 | tf_op jit(solution)/shard_map/all_gather | solution.py:47
  695.3 1.2 fusion.8
  696.6 1.3 constant_dynamic-update-slice_fusion.5
  698.6 1.3 constant_dynamic-update-slice_fusion.4
  699.9 109.0 %all-reduce.13.cloned.1.call-done = bf16[512,256]{0,1:T(8,128)(2,1)} async-done(((bf16[512,256]{0,1:T(8,128)(2,1)}), bf16[512,256]{0,1:T(8,128)(2,1)}) %all-reduce.13.cloned.1.call-update) | async-done | bytes 262160 | tf_op jit(solution)/shard_map/psum | solution.py:53
  808.9 1.5 fusion.13
  810.4 18.5 %all-gather.2 = bf16[512,256]{1,0:T(8,128)(2,1)S(1)} all-gather(bf16[32,256]{1,0:T(8,128)(2,1)S(1)} %fusion.13), channel_id=4, replica_groups=mesh['leaf'=16,'row'=16] {'leaf'}, dimensions={0}, use_global_device_ids=true | all-gather | bytes 278528 | tf_op jit(solution)/shard_map/all_gather | solution.py:47
  831.0 1.2 fusion.9
  832.3 1.6 dynamic-slice_bitcast_fusion.2
  833.9 1.5 copy.25
  836.1 1.3 constant_dynamic-update-slice_fusion.3
  837.5 107.2 %all-reduce.15.cloned.1.call-done = bf16[512,256]{0,1:T(8,128)(2,1)} async-done(((bf16[512,256]{0,1:T(8,128)(2,1)}), bf16[512,256]{0,1:T(8,128)(2,1)}) %all-reduce.15.cloned.1.call-update) | async-done | bytes 262160 | tf_op jit(solution)/shard_map/psum | solution.py:53
  944.7 1.4 fusion.14
  946.1 18.7 %all-gather.3 = bf16[512,256]{1,0:T(8,128)(2,1)S(1)} all-gather(bf16[32,256]{1,0:T(8,128)(2,1)S(1)} %fusion.14), channel_id=5, replica_groups=mesh['leaf'=16,'row'=16] {'leaf'}, dimensions={0}, use_global_device_ids=true | all-gather | bytes 278528 | tf_op jit(solution)/shard_map/all_gather | solution.py:47
  966.6 1.3 fusion.10
  969.6 110.7 %all-reduce.17.cloned.1.call-done = bf16[512,256]{0,1:T(8,128)(2,1)} async-done(((bf16[512,256]{0,1:T(8,128)(2,1)}), bf16[512,256]{0,1:T(8,128)(2,1)}) %all-reduce.17.cloned.1.call-update) | async-done | bytes 262160 | tf_op jit(solution)/shard_map/psum | solution.py:53
  1080.3 1.3 fusion.15
  1081.7 18.5 %all-gather.4 = bf16[512,256]{1,0:T(8,128)(2,1)S(1)} all-gather(bf16[32,256]{1,0:T(8,128)(2,1)S(1)} %fusion.15), channel_id=6, replica_groups=mesh['leaf'=16,'row'=16] {'leaf'}, dimensions={0}, use_global_device_ids=true | all-gather | bytes 278528 | tf_op jit(solution)/shard_map/all_gather | solution.py:47
  1101.3 1.3 fusion.7
  1103.9 111.1 %all-reduce.19.cloned.1.call-done = bf16[512,256]{0,1:T(8,128)(2,1)} async-done(((bf16[512,256]{0,1:T(8,128)(2,1)}), bf16[512,256]{0,1:T(8,128)(2,1)}) %all-reduce.19.cloned.1.call-update) | async-done | bytes 262160 | tf_op jit(solution)/shard_map/psum | solution.py:53
  1215.0 1.3 fusion.18
  (170 shorter events, 31.9 us)
Async XLA Ops:
  7.2 102.8 %reduce-scatter.16.cloned.1.call-start = ((), (), s32[]{:S(2)}) async-start(), calls=%async_computation.10 | async-start | bytes 278528
  8.0 24.6 %copy-start.31 = (f32[1,512]{1,0:T(1,128)}, f32[1,512]{1,0:T(1,128)S(1)}, u32[]{:S(2)}) copy-start(f32[1,512]{1,0:T(1,128)S(1)} %get-tuple-element.19) | copy-start | bytes 6148
  8.0 123.0 %copy-start.33 = (f32[1,512]{1,0:T(1,128)}, f32[1,512]{1,0:T(1,128)S(1)}, u32[]{:S(2)}) copy-start(f32[1,512]{1,0:T(1,128)S(1)} %get-tuple-element.18) | copy-start | bytes 6148
  8.0 227.1 %copy-start.35 = (f32[1,512]{1,0:T(1,128)}, f32[1,512]{1,0:T(1,128)S(1)}, u32[]{:S(2)}) copy-start(f32[1,512]{1,0:T(1,128)S(1)} %get-tuple-element.17) | copy-start | bytes 6148
  8.0 330.9 %copy-start.36 = (f32[1,512]{1,0:T(1,128)}, f32[1,512]{1,0:T(1,128)S(1)}, u32[]{:S(2)}) copy-start(f32[1,512]{1,0:T(1,128)S(1)} %get-tuple-element.16) | copy-start | bytes 6148
  8.0 434.6 %copy-start.37 = (f32[1,512]{1,0:T(1,128)}, f32[1,512]{1,0:T(1,128)S(1)}, u32[]{:S(2)}) copy-start(f32[1,512]{1,0:T(1,128)S(1)} %get-tuple-element.15) | copy-start | bytes 6148
  8.1 0.8 copy-start.38
  8.1 101.9 %copy-start.40 = (f32[32]{0:T(128)}, f32[32]{0:T(128)S(1)}, u32[]{:S(2)}) copy-start(f32[32]{0:T(128)S(1)} %get-tuple-element.24) | copy-start | bytes 388
  8.1 205.8 %copy-start.42 = (f32[32]{0:T(128)}, f32[32]{0:T(128)S(1)}, u32[]{:S(2)}) copy-start(f32[32]{0:T(128)S(1)} %get-tuple-element.23) | copy-start | bytes 388
  8.1 309.6 %copy-start.43 = (f32[32]{0:T(128)}, f32[32]{0:T(128)S(1)}, u32[]{:S(2)}) copy-start(f32[32]{0:T(128)S(1)} %get-tuple-element.22) | copy-start | bytes 388
  8.1 413.4 %copy-start.44 = (f32[32]{0:T(128)}, f32[32]{0:T(128)S(1)}, u32[]{:S(2)}) copy-start(f32[32]{0:T(128)S(1)} %get-tuple-element.21) | copy-start | bytes 388
  30.9 1.6 copy-start.46
  34.0 0.7 copy-start.10
  34.8 1.2 copy-start
  36.0 0.7 copy-start.21
  36.7 73.2 %copy-start.29 = (bf16[6,1,32,256]{3,2,1,0:T(8,128)(2,1)S(1)}, bf16[6,1,32,256]{3,2,1,0:T(8,128)(2,1)}, u32[]{:S(2)}) copy-start(bf16[6,1,32,256]{3,2,1,0:T(8,128)(2,1)} %param.5) | copy-start | bytes 294916
  36.7 177.2 %reduce-scatter.18.cloned.1.call-start = ((), (), s32[]{:S(2)}) async-start(), calls=%async_computation.11 | async-start | bytes 278528
  132.4 0.7 copy-start.12
  139.3 1.1 copy-start.1
  141.3 0.7 copy-start.22
  142.0 175.7 %reduce-scatter.20.cloned.1.call-start = ((), (), s32[]{:S(2)}) async-start(), calls=%async_computation.12 | async-start | bytes 278528
  213.9 23.3 %copy-start.2 = (bf16[1,40,32,512]{3,2,1,0:T(8,128)(2,1)S(1)}, bf16[1,40,32,512]{3,2,1,0:T(8,128)(2,1)}, u32[]{:S(2)}) copy-start(bf16[1,40,32,512]{3,2,1,0:T(8,128)(2,1)} %slice.238) | copy-start | bytes 3932164
  236.4 0.7 copy-start.16
  243.1 1.1 copy-start.4
  245.2 0.7 copy-start.20
  245.9 175.6 %reduce-scatter.22.cloned.1.call-start = ((), (), s32[]{:S(2)}) async-start(), calls=%async_computation.13 | async-start | bytes 278528
  317.7 23.2 %copy-start.7 = (bf16[1,32,32,512]{3,2,1,0:T(8,128)(2,1)S(1)}, bf16[1,32,32,512]{3,2,1,0:T(8,128)(2,1)}, u32[]{:S(2)}) copy-start(bf16[1,32,32,512]{3,2,1,0:T(8,128)(2,1)} %slice.249) | copy-start | bytes 3145732
  340.3 0.7 copy-start.15
  346.4 1.0 copy-start.9
  349.7 172.6 %reduce-scatter.24.cloned.1.call-start = ((), (), s32[]{:S(2)}) async-start(), calls=%async_computation.14 | async-start | bytes 278528
  350.9 95.0 %copy-start.5 = (bf16[1,16,32,512]{3,2,1,0:T(8,128)(2,1)}, bf16[1,16,32,512]{3,2,1,0:T(8,128)(2,1)S(1)}, u32[]{:S(2)}) copy-start(bf16[1,16,32,512]{3,2,1,0:T(8,128)(2,1)S(1)} %slice.261) | copy-start | bytes 1572868
  444.0 0.7 copy-start.13
  450.5 224.2 %all-reduce.11.cloned.1.call-start = ((), (), s32[]{:S(2)}) async-start(), calls=%async_computation.5 | async-start | bytes 524288 | tf_op jit(solution)/shard_map/psum | solution.py:53
  522.3 41.9 %copy-start.6 = (bf16[1,16,32,512]{3,2,1,0:T(8,128)(2,1)S(1)}, bf16[1,16,32,512]{3,2,1,0:T(8,128)(2,1)}, u32[]{:S(2)}) copy-start(bf16[1,16,32,512]{3,2,1,0:T(8,128)(2,1)} %copy-done.5) | copy-start | bytes 1572868
  544.8 19.2 %copy-start.24 = (bf16[256,512]{1,0:T(8,128)(2,1)}, bf16[256,512]{1,0:T(8,128)(2,1)S(1)}, u32[]{:S(2)}) copy-start(bf16[256,512]{1,0:T(8,128)(2,1)S(1)} %fusion.5) | copy-start | bytes 786436
  544.8 129.9 %copy-start.14 = (bf16[256,512]{1,0:T(8,128)(2,1)S(1)}, bf16[256,512]{1,0:T(8,128)(2,1)}, u32[]{:S(2)}) copy-start(bf16[256,512]{1,0:T(8,128)(2,1)} %copy-done.13) | copy-start | bytes 786436
  565.2 243.7 %all-reduce.13.cloned.1.call-start = ((), (), s32[]{:S(2)}) async-start(), calls=%async_computation.6 | async-start | bytes 524288 | tf_op jit(solution)/shard_map/psum | solution.py:53
  674.7 20.6 %copy-start.8 = (bf16[1,32,32,512]{3,2,1,0:T(8,128)(2,1)S(1)}, bf16[1,32,32,512]{3,2,1,0:T(8,128)(2,1)}, u32[]{:S(2)}) copy-start(bf16[1,32,32,512]{3,2,1,0:T(8,128)(2,1)} %slice.249) | copy-start | bytes 3145732
  676.1 18.5 %copy-start.25 = (bf16[32,256]{1,0:T(8,128)(2,1)}, bf16[32,256]{1,0:T(8,128)(2,1)S(1)}, u32[]{:S(2)}) copy-start(bf16[32,256]{1,0:T(8,128)(2,1)S(1)} %fusion.12) | copy-start | bytes 49156
  696.5 248.2 %all-reduce.15.cloned.1.call-start = ((), (), s32[]{:S(2)}) async-start(), calls=%async_computation.7 | async-start | bytes 524288 | tf_op jit(solution)/shard_map/psum | solution.py:53
  808.9 22.1 %copy-start.3 = (bf16[1,40,32,512]{3,2,1,0:T(8,128)(2,1)S(1)}, bf16[1,40,32,512]{3,2,1,0:T(8,128)(2,1)}, u32[]{:S(2)}) copy-start(bf16[1,40,32,512]{3,2,1,0:T(8,128)(2,1)} %slice.238) | copy-start | bytes 3932164
  810.4 21.8 %copy-start.27 = (bf16[32,256]{1,0:T(8,128)(2,1)}, bf16[32,256]{1,0:T(8,128)(2,1)S(1)}, u32[]{:S(2)}) copy-start(bf16[32,256]{1,0:T(8,128)(2,1)S(1)} %fusion.13) | copy-start | bytes 49156
  829.0 0.7 copy-start.18
  829.7 0.6 copy-start.17
  832.3 248.0 %all-reduce.17.cloned.1.call-start = ((), (), s32[]{:S(2)}) async-start(), calls=%async_computation.8 | async-start | bytes 524288 | tf_op jit(solution)/shard_map/psum | solution.py:53
  964.8 0.7 copy-start.23
  966.5 1.4 copy-start.30
  966.5 113.7 %copy-start.34 = (f32[1,512]{1,0:T(1,128)S(1)}, f32[1,512]{1,0:T(1,128)}, u32[]{:S(2)}) copy-start(f32[1,512]{1,0:T(1,128)} %copy-done.33) | copy-start | bytes 6148
  966.5 113.7 %copy-start.41 = (f32[32]{0:T(128)S(1)}, f32[32]{0:T(128)}, u32[]{:S(2)}) copy-start(f32[32]{0:T(128)} %copy-done.40) | copy-start | bytes 388
  967.8 133.2 %copy-start.19 = (bf16[512,256]{1,0:T(8,128)(2,1)S(1)}, bf16[512,256]{1,0:T(8,128)(2,1)}, u32[]{:S(2)}) copy-start(bf16[512,256]{1,0:T(8,128)(2,1)} %copy-done.18) | copy-start | bytes 786436
  967.9 133.2 %copy-start.47 = (bf16[46]{0:T(256)(128)(2,1)S(1)}, bf16[46]{0:T(256)(128)(2,1)}, u32[]{:S(2)}) copy-start(bf16[46]{0:T(256)(128)(2,1)} %slice_bitcast_fusion) | copy-start | bytes 280
  967.9 247.1 %all-reduce.19.cloned.1.call-start = ((), (), s32[]{:S(2)}) async-start(), calls=%async_computation.9 | async-start | bytes 524288 | tf_op jit(solution)/shard_map/psum | solution.py:53
  1101.2 113.8 %copy-start.11 = (bf16[256,512]{1,0:T(8,128)(2,1)S(1)}, bf16[256,512]{1,0:T(8,128)(2,1)}, u32[]{:S(2)}) copy-start(bf16[256,512]{1,0:T(8,128)(2,1)} %copy-done.10) | copy-start | bytes 786436
  1101.2 113.8 %copy-start.32 = (f32[1,512]{1,0:T(1,128)S(1)}, f32[1,512]{1,0:T(1,128)}, u32[]{:S(2)}) copy-start(f32[1,512]{1,0:T(1,128)} %copy-done.31) | copy-start | bytes 6148
  1101.3 113.8 %copy-start.39 = (f32[32]{0:T(128)S(1)}, f32[32]{0:T(128)}, u32[]{:S(2)}) copy-start(f32[32]{0:T(128)} %copy-done.38) | copy-start | bytes 388
  1101.3 115.1 %copy-start.28 = (bf16[32,256]{1,0:T(8,128)(2,1)S(1)}, bf16[32,256]{1,0:T(8,128)(2,1)}, u32[]{:S(2)}) copy-start(bf16[32,256]{1,0:T(8,128)(2,1)} %copy-done.27) | copy-start | bytes 49156
  1101.3 115.1 %copy-start.26 = (bf16[32,256]{1,0:T(8,128)(2,1)S(1)}, bf16[32,256]{1,0:T(8,128)(2,1)}, u32[]{:S(2)}) copy-start(bf16[32,256]{1,0:T(8,128)(2,1)} %copy-done.25) | copy-start | bytes 49156
  1216.4 0.6 copy-start.45
Sparse Core Ops, SparseCore 0:
  36.8 73.0 reduce-scatter.15
  142.2 71.6 reduce-scatter.17
  246.1 71.6 reduce-scatter.19
  349.8 71.6 reduce-scatter.21
  450.6 71.6 reduce-scatter.23
  565.4 109.3 all-reduce.10
  696.6 112.2 all-reduce.12
  832.4 112.2 all-reduce.14
  968.0 112.2 all-reduce.16
  1102.7 112.2 all-reduce.18
where the time goes:
time: 1230 us; the launch traced here: 1220 us
  waiting for transfers between devices  891 us (72%)
  blocking collectives  215 us (17%)
  local copies, waits for them, and re-layouts  53.4 us (4%)
  matrix products  29 us (2%)
  other arithmetic  19.6 us (2%)
  between operations  15 us (1%)
    psum x5, waiting for transfers between devices, adjoint_level(): lax.psum(contract_rows(flat_blocks, flat_values).astype(jnp.bfloat16), 'r...  544 us
    unnamed x15, waiting for transfers between devices  347 us
    all_gather x6, blocking collectives, shards(): lax.all_gather(residual, 'row', axis=0, tiled=True)  123 us
    all_gather x5, blocking collectives, group_collect(): everyone = lax.all_gather(own_block[None], 'leaf', axis=0, tiled=True)  92.2 us
  transfers between devices with their start and end apart: 10, of which 10 were waited for; matrix products, arithmetic and copies ran while one was open for 2% of the time, Pallas kernels for 0%

commit v1 on v0

--- a/solution.py
+++ b/solution.py
@@ -1,7 +1,21 @@
+import functools
 import jax
 import jax.numpy as jnp
 from jax import lax
 from jax.sharding import PartitionSpec as P
+
+
+def update_array(state, axis_id):
+    out_arr = jnp.concatenate(
+        lax.all_to_all(
+            jnp.stack([state for _ in range(lax.psum(1, axis_id))], axis=0), axis_id, 0, 0
+        ),
+        axis=0,
+    )
+    return out_arr
+
+
+search_page = functools.partial(update_array, axis_id="row")
 
 
 def group_size(level_now, leaf_count):
@@ -94,7 +108,7 @@
             block_masks[level_now][:, None] * (rhs[level_now, 0].astype(jnp.float32) - incoming)
         ).astype(jnp.bfloat16)
         solve_rows = inverse[level_now]
-        folded = apply_columns(solve_rows, lax.all_gather(residual, "row", axis=0, tiled=True))
+        folded = apply_columns(solve_rows, search_page(residual))
         solved_full = (full_masks[level_now][:, None] * folded).astype(jnp.bfloat16)
         solved_block = lax.dynamic_slice_in_dim(solved_full, own_rows, block_rows, 0)
         forward_blocks.append(solved_block)

time: 1230 us -> 1220 us (level)
  blocking collectives: 215 us -> 91.9 us
  waiting for transfers between devices: 891 us -> 949 us
  starting transfers between devices: 0.41 us -> 57.1 us
    all_gather x6 -> x0, blocking collectives: 123 us -> none  [shards(): lax.all_gather(residual, 'row', axis=0, tiled=True)]
    all_to_all x0 -> x6, starting transfers between devices: none -> 56.5 us  [update_array(): lax.all_to_all(jnp.stack([state for _ in range(lax.psum(1, axis_id))], ax...]
    all_to_all x0 -> x6, waiting for transfers between devices: none -> 55.7 us  [update_array(): lax.all_to_all(jnp.stack([state for _ in range(lax.psum(1, axis_id))], ax...]
  transfers between devices with their start and end apart: 10 -> 16, of which waited for: 10 -> 16; matrix products, arithmetic and copies ran while one was open for 2% -> 3% of each run, Pallas kernels for 0% -> 0%
where the time goes in v1:
time: 1220 us
  waiting for transfers between devices  949 us (78%)
  blocking collectives  91.9 us (8%)
  local copies, waits for them, and re-layouts  57.7 us (5%)
  starting transfers between devices  57.1 us (5%)
  matrix products  30.6 us (3%)
  other arithmetic  20.1 us (2%)
  between operations  15 us (1%)
    psum x5, waiting for transfers between devices, adjoint_level(): lax.psum(contract_rows(flat_blocks, flat_values).astype(jnp.bfloat16), 'r...  542 us
    unnamed x15, waiting for transfers between devices  352 us
    all_gather x5, blocking collectives, group_collect(): everyone = lax.all_gather(own_block[None], 'leaf', axis=0, tiled=True)  91.9 us
    all_to_all x6, starting transfers between devices, update_array(): lax.all_to_all(jnp.stack([state for _ in range(lax.psum(1, axis_id))], ax...  56.5 us
    all_to_all x6, waiting for transfers between devices, update_array(): lax.all_to_all(jnp.stack([state for _ in range(lax.psum(1, axis_id))], ax...  55.7 us
  transfers between devices with their start and end apart: 16, of which 16 were waited for; matrix products, arithmetic and copies ran while one was open for 3% of the time, Pallas kernels for 0%

profile of v1, /device:TPU:1, one launch (start us, length us, event | category | flops | bytes accessed | tf_op | source)
XLA Modules:
  0.0 1221.8 jit_solution(7019565486835438566)
XLA Ops:
  9.6 10.0 all-to-all-start
  20.3 1.5 slice.230
  22.0 9.3 all-to-all-done
  31.2 1.4 fusion
  35.4 72.3 %reduce-scatter.16.cloned.1.call-done = bf16[1,32,256]{2,1,0:T(8,128)(2,1)} async-done(((bf16[16,32,256]{2,1,0:T(8,128)(2,1)}), bf16[1,32,256]{2,1,0:T(8,128)(2,1)}) %reduce-scatter.16.cloned.1.call-update) | async-done | bytes 16400
  109.2 9.3 all-to-all-start.1
  118.5 1.5 slice.240
  120.2 10.1 all-to-all-done.1
  130.2 1.4 fusion.1
  132.3 1.7 convolution_bitcast_fusion.1
  134.0 2.9 copy.19
  136.9 1.5 broadcast_multiply_fusion.1
  141.2 70.3 %reduce-scatter.18.cloned.1.call-done = bf16[1,32,256]{2,1,0:T(8,128)(2,1)} async-done(((bf16[16,32,256]{2,1,0:T(8,128)(2,1)}), bf16[1,32,256]{2,1,0:T(8,128)(2,1)}) %reduce-scatter.18.cloned.1.call-update) | async-done | bytes 16400
  213.0 9.3 all-to-all-start.2
  222.3 2.5 slice.251
  224.9 9.1 all-to-all-done.2
  234.0 1.4 fusion.2
  236.1 3.0 convolution_bitcast_fusion
  239.0 2.8 copy.20
  241.8 1.5 broadcast_multiply_fusion.2
  246.2 70.0 %reduce-scatter.20.cloned.1.call-done = bf16[1,32,256]{2,1,0:T(8,128)(2,1)} async-done(((bf16[16,32,256]{2,1,0:T(8,128)(2,1)}), bf16[1,32,256]{2,1,0:T(8,128)(2,1)}) %reduce-scatter.20.cloned.1.call-update) | async-done | bytes 16400
  317.7 9.3 all-to-all-start.3
  327.1 2.3 slice.263
  329.5 9.3 all-to-all-done.3
  338.8 1.5 fusion.3
  340.9 1.5 convolution_bitcast_fusion.2
  342.5 2.6 copy.21
  345.1 1.4 broadcast_multiply_fusion.3
  347.5 2.2 fusion.21
  349.8 70.1 %reduce-scatter.22.cloned.1.call-done = bf16[1,32,256]{2,1,0:T(8,128)(2,1)} async-done(((bf16[16,32,256]{2,1,0:T(8,128)(2,1)}), bf16[1,32,256]{2,1,0:T(8,128)(2,1)}) %reduce-scatter.22.cloned.1.call-update) | async-done | bytes 16400
  421.3 9.3 all-to-all-start.4
  431.9 10.6 all-to-all-done.4
  442.5 1.5 fusion.4
  445.8 2.1 copy.22
  447.8 2.5 fusion.20
  451.6 69.0 %reduce-scatter.24.cloned.1.call-done = bf16[1,32,256]{2,1,0:T(8,128)(2,1)} async-done(((bf16[16,32,256]{2,1,0:T(8,128)(2,1)}), bf16[1,32,256]{2,1,0:T(8,128)(2,1)}) %reduce-scatter.24.cloned.1.call-update) | async-done | bytes 16400
  522.1 9.3 all-to-all-start.5
  532.1 3.6 fusion.91
  535.6 7.5 all-to-all-done.5
  543.1 1.4 fusion.5
  545.8 17.8 %all-gather = bf16[512,256]{1,0:T(8,128)(2,1)S(1)} all-gather(bf16[32,256]{1,0:T(8,128)(2,1)S(1)} %fusion.11), channel_id=2, replica_groups=mesh['leaf'=16,'row'=16] {'leaf'}, dimensions={0}, use_global_device_ids=true | all-gather | bytes 278528 | tf_op jit(solution)/shard_map/all_gather | solution.py:61
  565.5 1.6 dynamic-slice_bitcast_fusion.4
  567.1 1.5 copy.23
  568.6 104.0 %all-reduce.11.cloned.1.call-done = bf16[512,256]{0,1:T(8,128)(2,1)} async-done(((bf16[512,256]{0,1:T(8,128)(2,1)}), bf16[512,256]{0,1:T(8,128)(2,1)}) %all-reduce.11.cloned.1.call-update) | async-done | bytes 262160 | tf_op jit(solution)/shard_map/psum | solution.py:67
  672.7 1.3 fusion.12
  674.0 18.5 %all-gather.1 = bf16[512,256]{1,0:T(8,128)(2,1)S(1)} all-gather(bf16[32,256]{1,0:T(8,128)(2,1)S(1)} %fusion.12), channel_id=3, replica_groups=mesh['leaf'=16,'row'=16] {'leaf'}, dimensions={0}, use_global_device_ids=true | all-gather | bytes 278528 | tf_op jit(solution)/shard_map/all_gather | solution.py:61
  694.5 1.3 constant_dynamic-update-slice_fusion.5
  696.5 1.3 constant_dynamic-update-slice_fusion.4
  697.8 109.0 %all-reduce.13.cloned.1.call-done = bf16[512,256]{0,1:T(8,128)(2,1)} async-done(((bf16[512,256]{0,1:T(8,128)(2,1)}), bf16[512,256]{0,1:T(8,128)(2,1)}) %all-reduce.13.cloned.1.call-update) | async-done | bytes 262160 | tf_op jit(solution)/shard_map/psum | solution.py:67
  806.9 1.5 fusion.13
  808.4 18.5 %all-gather.2 = bf16[512,256]{1,0:T(8,128)(2,1)S(1)} all-gather(bf16[32,256]{1,0:T(8,128)(2,1)S(1)} %fusion.13), channel_id=4, replica_groups=mesh['leaf'=16,'row'=16] {'leaf'}, dimensions={0}, use_global_device_ids=true | all-gather | bytes 278528 | tf_op jit(solution)/shard_map/all_gather | solution.py:61
  830.5 1.6 dynamic-slice_bitcast_fusion.2
  832.1 1.5 copy.25
  834.3 1.3 constant_dynamic-update-slice_fusion.3
  835.7 107.0 %all-reduce.15.cloned.1.call-done = bf16[512,256]{0,1:T(8,128)(2,1)} async-done(((bf16[512,256]{0,1:T(8,128)(2,1)}), bf16[512,256]{0,1:T(8,128)(2,1)}) %all-reduce.15.cloned.1.call-update) | async-done | bytes 262160 | tf_op jit(solution)/shard_map/psum | solution.py:67
  942.7 1.4 fusion.14
  944.1 18.5 %all-gather.3 = bf16[512,256]{1,0:T(8,128)(2,1)S(1)} all-gather(bf16[32,256]{1,0:T(8,128)(2,1)S(1)} %fusion.14), channel_id=5, replica_groups=mesh['leaf'=16,'row'=16] {'leaf'}, dimensions={0}, use_global_device_ids=true | all-gather | bytes 278528 | tf_op jit(solution)/shard_map/all_gather | solution.py:61
  964.4 1.3 fusion.10
  967.4 110.7 %all-reduce.17.cloned.1.call-done = bf16[512,256]{0,1:T(8,128)(2,1)} async-done(((bf16[512,256]{0,1:T(8,128)(2,1)}), bf16[512,256]{0,1:T(8,128)(2,1)}) %all-reduce.17.cloned.1.call-update) | async-done | bytes 262160 | tf_op jit(solution)/shard_map/psum | solution.py:67
  1078.1 1.3 fusion.15
  1079.5 18.5 %all-gather.4 = bf16[512,256]{1,0:T(8,128)(2,1)S(1)} all-gather(bf16[32,256]{1,0:T(8,128)(2,1)S(1)} %fusion.15), channel_id=6, replica_groups=mesh['leaf'=16,'row'=16] {'leaf'}, dimensions={0}, use_global_device_ids=true | all-gather | bytes 278528 | tf_op jit(solution)/shard_map/all_gather | solution.py:61
  1099.1 1.3 fusion.7
  1101.8 111.1 %all-reduce.19.cloned.1.call-done = bf16[512,256]{0,1:T(8,128)(2,1)} async-done(((bf16[512,256]{0,1:T(8,128)(2,1)}), bf16[512,256]{0,1:T(8,128)(2,1)}) %all-reduce.19.cloned.1.call-update) | async-done | bytes 262160 | tf_op jit(solution)/shard_map/psum | solution.py:67
  1212.9 1.3 fusion.18
  (178 shorter events, 43.9 us)
Async XLA Ops:
  8.0 13.9 %copy-start.37 = (f32[32]{0:T(128)}, f32[32]{0:T(128)S(1)}, u32[]{:S(2)}) copy-start(f32[32]{0:T(128)S(1)} %get-tuple-element.25) | copy-start | bytes 388
  8.0 99.7 %copy-start.39 = (f32[32]{0:T(128)}, f32[32]{0:T(128)S(1)}, u32[]{:S(2)}) copy-start(f32[32]{0:T(128)S(1)} %get-tuple-element.24) | copy-start | bytes 388
  8.0 203.5 %copy-start.41 = (f32[32]{0:T(128)}, f32[32]{0:T(128)S(1)}, u32[]{:S(2)}) copy-start(f32[32]{0:T(128)S(1)} %get-tuple-element.23) | copy-start | bytes 388
  8.0 308.2 %copy-start.42 = (f32[32]{0:T(128)}, f32[32]{0:T(128)S(1)}, u32[]{:S(2)}) copy-start(f32[32]{0:T(128)S(1)} %get-tuple-element.22) | copy-start | bytes 388
  8.0 411.8 %copy-start.43 = (f32[32]{0:T(128)}, f32[32]{0:T(128)S(1)}, u32[]{:S(2)}) copy-start(f32[32]{0:T(128)S(1)} %get-tuple-element.21) | copy-start | bytes 388
  9.6 21.7 %all-to-all-start = ((bf16[16,32,256]{2,1,0:T(8,128)(2,1)}), bf16[16,32,256]{2,1,0:T(8,128)(2,1)S(1)}, u32[]{:S(2)}, u32[]{:S(2)}) async-start(bf16[16,32,256]{2,1,0:T(8,128)(2,1)} %stack.40), calls=%async_computation | async-start | bytes 524288 | tf_op jit(solution)/shard_map/all_to_all | solution.py:10
  19.5 88.1 %reduce-scatter.16.cloned.1.call-start = ((), (), s32[]{:S(2)}) async-start(), calls=%async_computation.16 | async-start | bytes 278528
  21.9 11.3 copy-start.30
  21.9 108.3 %copy-start.32 = (f32[1,512]{1,0:T(1,128)}, f32[1,512]{1,0:T(1,128)S(1)}, u32[]{:S(2)}) copy-start(f32[1,512]{1,0:T(1,128)S(1)} %get-tuple-element.18) | copy-start | bytes 6148
  22.0 212.0 %copy-start.34 = (f32[1,512]{1,0:T(1,128)}, f32[1,512]{1,0:T(1,128)S(1)}, u32[]{:S(2)}) copy-start(f32[1,512]{1,0:T(1,128)S(1)} %get-tuple-element.17) | copy-start | bytes 6148
  22.0 316.8 %copy-start.35 = (f32[1,512]{1,0:T(1,128)}, f32[1,512]{1,0:T(1,128)S(1)}, u32[]{:S(2)}) copy-start(f32[1,512]{1,0:T(1,128)S(1)} %get-tuple-element.16) | copy-start | bytes 6148
  22.0 420.5 %copy-start.36 = (f32[1,512]{1,0:T(1,128)}, f32[1,512]{1,0:T(1,128)S(1)}, u32[]{:S(2)}) copy-start(f32[1,512]{1,0:T(1,128)S(1)} %get-tuple-element.15) | copy-start | bytes 6148
  32.6 0.7 copy-start.9
  33.3 74.3 %copy-start.28 = (bf16[6,1,32,256]{3,2,1,0:T(8,128)(2,1)S(1)}, bf16[6,1,32,256]{3,2,1,0:T(8,128)(2,1)}, u32[]{:S(2)}) copy-start(bf16[6,1,32,256]{3,2,1,0:T(8,128)(2,1)} %param.5) | copy-start | bytes 294916
  33.5 1.2 copy-start
  34.7 0.7 copy-start.20
  109.2 21.0 %all-to-all-start.1 = ((bf16[16,32,256]{2,1,0:T(8,128)(2,1)}), bf16[16,32,256]{2,1,0:T(8,128)(2,1)S(1)}, u32[]{:S(2)}, u32[]{:S(2)}) async-start(bf16[16,32,256]{2,1,0:T(8,128)(2,1)} %stack.43), calls=%async_computation.1 | async-start | bytes 524288 | tf_op jit(solution)/shard_map/all_to_all | solution.py:10
  118.5 92.9 %reduce-scatter.18.cloned.1.call-start = ((), (), s32[]{:S(2)}) async-start(), calls=%async_computation.17 | async-start | bytes 278528
  131.6 0.7 copy-start.11
  138.4 1.1 copy-start.1
  140.5 0.7 copy-start.21
  213.0 21.0 %all-to-all-start.2 = ((bf16[16,32,256]{2,1,0:T(8,128)(2,1)}), bf16[16,32,256]{2,1,0:T(8,128)(2,1)S(1)}, u32[]{:S(2)}, u32[]{:S(2)}) async-start(bf16[16,32,256]{2,1,0:T(8,128)(2,1)} %stack.46), calls=%async_computation.2 | async-start | bytes 524288 | tf_op jit(solution)/shard_map/all_to_all | solution.py:10
  222.3 94.0 %reduce-scatter.20.cloned.1.call-start = ((), (), s32[]{:S(2)}) async-start(), calls=%async_computation.18 | async-start | bytes 278528
  235.4 0.7 copy-start.15
  243.3 1.1 copy-start.3
  245.4 0.7 copy-start.19
  317.7 21.0 %all-to-all-start.3 = ((bf16[16,32,256]{2,1,0:T(8,128)(2,1)}), bf16[16,32,256]{2,1,0:T(8,128)(2,1)S(1)}, u32[]{:S(2)}, u32[]{:S(2)}) async-start(bf16[16,32,256]{2,1,0:T(8,128)(2,1)} %stack.49), calls=%async_computation.3 | async-start | bytes 524288 | tf_op jit(solution)/shard_map/all_to_all | solution.py:10
  327.0 92.8 %reduce-scatter.22.cloned.1.call-start = ((), (), s32[]{:S(2)}) async-start(), calls=%async_computation.19 | async-start | bytes 278528
  338.7 2.2 copy-start.6
  340.2 0.7 copy-start.14
  346.5 1.1 copy-start.8
  421.3 21.1 %all-to-all-start.4 = ((bf16[16,32,256]{2,1,0:T(8,128)(2,1)}), bf16[16,32,256]{2,1,0:T(8,128)(2,1)}, u32[]{:S(2)}, u32[]{:S(2)}) async-start(bf16[16,32,256]{2,1,0:T(8,128)(2,1)} %stack.52), calls=%async_computation.4 | async-start | bytes 524288 | tf_op jit(solution)/shard_map/all_to_all | solution.py:10
  430.6 89.9 %reduce-scatter.24.cloned.1.call-start = ((), (), s32[]{:S(2)}) async-start(), calls=%async_computation.20 | async-start | bytes 278528
  431.8 16.1 %copy-start.4 = (bf16[1,16,32,512]{3,2,1,0:T(8,128)(2,1)}, bf16[1,16,32,512]{3,2,1,0:T(8,128)(2,1)S(1)}, u32[]{:S(2)}) copy-start(bf16[1,16,32,512]{3,2,1,0:T(8,128)(2,1)S(1)} %slice.276) | copy-start | bytes 1572868
  443.9 0.7 copy-start.12
  522.1 21.0 %all-to-all-start.5 = ((bf16[16,32,256]{2,1,0:T(8,128)(2,1)}), bf16[16,32,256]{2,1,0:T(8,128)(2,1)S(1)}, u32[]{:S(2)}, u32[]{:S(2)}) async-start(bf16[16,32,256]{2,1,0:T(8,128)(2,1)} %stack.55), calls=%async_computation.5 | async-start | bytes 524288 | tf_op jit(solution)/shard_map/all_to_all | solution.py:10
  531.4 141.2 %all-reduce.11.cloned.1.call-start = ((), (), s32[]{:S(2)}) async-start(), calls=%async_computation.11 | async-start | bytes 524288 | tf_op jit(solution)/shard_map/psum | solution.py:67
  543.1 20.7 %copy-start.5 = (bf16[1,16,32,512]{3,2,1,0:T(8,128)(2,1)S(1)}, bf16[1,16,32,512]{3,2,1,0:T(8,128)(2,1)}, u32[]{:S(2)}) copy-start(bf16[1,16,32,512]{3,2,1,0:T(8,128)(2,1)} %copy-done.4) | copy-start | bytes 1572868
  544.6 19.1 %copy-start.23 = (bf16[256,512]{1,0:T(8,128)(2,1)}, bf16[256,512]{1,0:T(8,128)(2,1)S(1)}, u32[]{:S(2)}) copy-start(bf16[256,512]{1,0:T(8,128)(2,1)S(1)} %fusion.5) | copy-start | bytes 786436
  544.6 128.1 %copy-start.13 = (bf16[256,512]{1,0:T(8,128)(2,1)S(1)}, bf16[256,512]{1,0:T(8,128)(2,1)}, u32[]{:S(2)}) copy-start(bf16[256,512]{1,0:T(8,128)(2,1)} %copy-done.12) | copy-start | bytes 786436
  564.9 242.0 %all-reduce.13.cloned.1.call-start = ((), (), s32[]{:S(2)}) async-start(), calls=%async_computation.12 | async-start | bytes 524288 | tf_op jit(solution)/shard_map/psum | solution.py:67
  672.6 20.6 %copy-start.7 = (bf16[1,32,32,512]{3,2,1,0:T(8,128)(2,1)S(1)}, bf16[1,32,32,512]{3,2,1,0:T(8,128)(2,1)}, u32[]{:S(2)}) copy-start(bf16[1,32,32,512]{3,2,1,0:T(8,128)(2,1)} %slice.263) | copy-start | bytes 3145732
  674.0 18.5 %copy-start.24 = (bf16[32,256]{1,0:T(8,128)(2,1)}, bf16[32,256]{1,0:T(8,128)(2,1)S(1)}, u32[]{:S(2)}) copy-start(bf16[32,256]{1,0:T(8,128)(2,1)S(1)} %fusion.12) | copy-start | bytes 49156
  694.4 248.3 %all-reduce.15.cloned.1.call-start = ((), (), s32[]{:S(2)}) async-start(), calls=%async_computation.13 | async-start | bytes 524288 | tf_op jit(solution)/shard_map/psum | solution.py:67
  806.9 22.1 %copy-start.2 = (bf16[1,40,32,512]{3,2,1,0:T(8,128)(2,1)S(1)}, bf16[1,40,32,512]{3,2,1,0:T(8,128)(2,1)}, u32[]{:S(2)}) copy-start(bf16[1,40,32,512]{3,2,1,0:T(8,128)(2,1)} %slice.251) | copy-start | bytes 3932164
  808.3 21.9 %copy-start.26 = (bf16[32,256]{1,0:T(8,128)(2,1)}, bf16[32,256]{1,0:T(8,128)(2,1)S(1)}, u32[]{:S(2)}) copy-start(bf16[32,256]{1,0:T(8,128)(2,1)S(1)} %fusion.13) | copy-start | bytes 49156
  826.9 0.7 copy-start.17
  827.6 0.7 copy-start.16
  830.3 247.8 %all-reduce.17.cloned.1.call-start = ((), (), s32[]{:S(2)}) async-start(), calls=%async_computation.14 | async-start | bytes 524288 | tf_op jit(solution)/shard_map/psum | solution.py:67
  962.6 0.7 copy-start.22
  964.4 1.4 copy-start.29
  964.4 113.8 %copy-start.33 = (f32[1,512]{1,0:T(1,128)S(1)}, f32[1,512]{1,0:T(1,128)}, u32[]{:S(2)}) copy-start(f32[1,512]{1,0:T(1,128)} %copy-done.32) | copy-start | bytes 6148
  964.4 113.8 %copy-start.40 = (f32[32]{0:T(128)S(1)}, f32[32]{0:T(128)}, u32[]{:S(2)}) copy-start(f32[32]{0:T(128)} %copy-done.39) | copy-start | bytes 388
  965.7 133.2 %copy-start.18 = (bf16[512,256]{1,0:T(8,128)(2,1)S(1)}, bf16[512,256]{1,0:T(8,128)(2,1)}, u32[]{:S(2)}) copy-start(bf16[512,256]{1,0:T(8,128)(2,1)} %copy-done.17) | copy-start | bytes 786436
  965.7 133.3 %copy-start.45 = (bf16[46]{0:T(256)(128)(2,1)S(1)}, bf16[46]{0:T(256)(128)(2,1)}, u32[]{:S(2)}) copy-start(bf16[46]{0:T(256)(128)(2,1)} %slice_bitcast_fusion) | copy-start | bytes 280
  965.7 247.2 %all-reduce.19.cloned.1.call-start = ((), (), s32[]{:S(2)}) async-start(), calls=%async_computation.15 | async-start | bytes 524288 | tf_op jit(solution)/shard_map/psum | solution.py:67
  1099.1 113.8 %copy-start.10 = (bf16[256,512]{1,0:T(8,128)(2,1)S(1)}, bf16[256,512]{1,0:T(8,128)(2,1)}, u32[]{:S(2)}) copy-start(bf16[256,512]{1,0:T(8,128)(2,1)} %copy-done.9) | copy-start | bytes 786436
  1099.1 113.8 %copy-start.31 = (f32[1,512]{1,0:T(1,128)S(1)}, f32[1,512]{1,0:T(1,128)}, u32[]{:S(2)}) copy-start(f32[1,512]{1,0:T(1,128)} %copy-done.30) | copy-start | bytes 6148
  1099.1 113.8 %copy-start.38 = (f32[32]{0:T(128)S(1)}, f32[32]{0:T(128)}, u32[]{:S(2)}) copy-start(f32[32]{0:T(128)} %copy-done.37) | copy-start | bytes 388
  1099.1 115.1 %copy-start.27 = (bf16[32,256]{1,0:T(8,128)(2,1)S(1)}, bf16[32,256]{1,0:T(8,128)(2,1)}, u32[]{:S(2)}) copy-start(bf16[32,256]{1,0:T(8,128)(2,1)} %copy-done.26) | copy-start | bytes 49156
  1099.1 115.1 %copy-start.25 = (bf16[32,256]{1,0:T(8,128)(2,1)S(1)}, bf16[32,256]{1,0:T(8,128)(2,1)}, u32[]{:S(2)}) copy-start(bf16[32,256]{1,0:T(8,128)(2,1)} %copy-done.24) | copy-start | bytes 49156
  1214.3 0.6 copy-start.44
Sparse Core Ops, SparseCore 0:
  35.5 72.1 reduce-scatter.15
  141.3 70.0 reduce-scatter.17
  246.3 69.8 reduce-scatter.19
  349.9 69.9 reduce-scatter.21
  450.5 70.0 reduce-scatter.23
  565.0 107.6 all-reduce.10
  694.6 112.2 all-reduce.12
  830.4 112.2 all-reduce.14
  965.8 112.2 all-reduce.16
  1100.6 112.2 all-reduce.18
